TPU v7x, 32 devices: a whole 2x2x4 slice. The times are simulated.
32 devices in a mesh: ctx: 16 (over z, y, x), head: 2 (over core).
Axes of the slice: x: 2, y: 2, z: 4, core: 2. Of those that a mesh axis runs over, the one named last changes fastest.
Arguments:
- obs_query: bfloat16 [256, 5120], P('ctx', 'head'), may hold values from -80 to 80
- prefix_keys: bfloat16 [16384, 1024], P('ctx', 'head'), may hold values from -8 to 8
- prefix_values: bfloat16 [16384, 1024], P('ctx', 'head'), may hold values from -4 to 4
- dec_query: bfloat16 [64, 5120], P(None, 'head'), may hold values from -80 to 80
- kept_pages: int32 [16, 16, 2], P(None, 'ctx'), may hold values from 0 to 7, as said below
- page_counts: int32 [16, 16], replicated, may hold values from 0 to 2, as said below
- assignment: int32 [64], replicated, may hold values from 0 to 63, each once
Outputs:
- token_scores: float32 [4, 16384], P(None, ('ctx', 'head'))
- decode_out: bfloat16 [64, 5120], P('ctx', 'head')
Inputs may be any that keep to these rules, and one draw needn't show every extreme that they name: kept_pages[p, o, j] is the index, among the 8 pages of the context shard at ctx index o, of the page that replica p keeps in slot j; a slot holds a kept page only if j < page_counts[p, o]; the two slots of one p and o name different pages; slot 0 of shard 0 is page 0 for every replica. page_counts[p, o] counts the pages replica p keeps from shard o; it is at least 1 for shard 0, and some replica keeps 2 pages from every shard.
All inputs are finite; a program needn't handle non-finite values.
Results may differ from a plain program's by a relative error of at most 0.0012.
Values may be sent and summed in bfloat16 or wider, within the bound.
A program may use at most 64 MiB of HBM per device.

v0:
```python
import math

import jax
import jax.numpy as jnp
from jax import lax
from jax.sharding import PartitionSpec as P

QH = 40
HD = 128
OBS = 64
POOL = 7
PAGE = 128
CAP = 2
SLOTS = 4
G = 5


masked_low = -1e30


def combined_all(part, axis, combine):
    gathered = jax.tree.map(lambda a: lax.all_gather(a, axis), part)

    def take(source):
        return jax.tree.map(lambda a: lax.dynamic_index_in_dim(a, source, 0, False), gathered)

    return lax.fori_loop(
        1, lax.axis_size(axis), lambda source, state: combine(state, take(source)), take(0)
    )


def extended(x, sides, width):
    for axis, dim in sides:
        size, length = (lax.axis_size(axis), x.shape[dim])
        up = [(i, (i + 1) % size) for i in range(size - 1)]
        down = [(j, i) for i, j in up]
        last = lax.slice_in_dim(x, length - width, length, axis=dim)
        initial = lax.slice_in_dim(x, 0, width, axis=dim)
        before = lax.ppermute(last, axis, up)
        after = lax.ppermute(initial, axis, down)
        x = jnp.concatenate([before, x, after], axis=dim)
    return x


def window_sum(padded, span_len):
    running = padded[:, 0:span_len]
    for offset in range(1, POOL):
        running = running + padded[:, offset : offset + span_len]
    return running


def merge_stats(former, latter):
    joint_max = jnp.maximum(former[0], latter[0])
    joint_sum = former[1] * jnp.exp(former[0] - joint_max) + latter[1] * jnp.exp(
        latter[0] - joint_max
    )
    return (joint_max, joint_sum)


def local(obs_query, prefix_keys, prefix_values, dec_query, kept_pages, page_counts, assignment):
    score_scale = 1.0 / math.sqrt(HD)
    ctx_len = prefix_keys.shape[0]
    heads_local = prefix_keys.shape[1] // HD
    gathered = lax.all_gather(obs_query, "ctx", axis=0, tiled=True)
    row_count = gathered.shape[0]
    requests_all = row_count // OBS
    queries = jnp.transpose(gathered.reshape(row_count, heads_local, G, HD), (1, 2, 0, 3)).reshape(
        heads_local, G * row_count, HD
    )
    key_rows = prefix_keys.reshape(ctx_len, heads_local, HD)
    block_len = math.gcd(512, ctx_len)
    starts = jnp.arange(ctx_len // block_len, dtype=jnp.int32) * block_len

    def block_scores(offset):
        key_block = lax.dynamic_slice_in_dim(key_rows, offset, block_len, 0)
        return (
            jnp.einsum("hqd,thd->hqt", queries, key_block, preferred_element_type=jnp.float32)
            * score_scale
        )

    def stats_step(running, offset):
        run_max, run_sum = running
        scores = block_scores(offset)
        new_max = jnp.maximum(run_max, jnp.max(scores, axis=2))
        new_sum = run_sum * jnp.exp(run_max - new_max) + jnp.sum(
            jnp.exp(scores - new_max[:, :, None]), axis=2
        )
        return ((new_max, new_sum), None)

    start_max = jnp.full((heads_local, G * row_count), -jnp.inf, jnp.float32)
    start_sum = jnp.zeros((heads_local, G * row_count), jnp.float32)
    (local_max, local_sum), _ = lax.scan(stats_step, (start_max, start_sum), starts)
    row_max, row_sum = combined_all((local_max, local_sum), "ctx", merge_stats)

    def weight_step(unused, offset):
        scores = block_scores(offset)
        weights = jnp.exp(scores - row_max[:, :, None]) / row_sum[:, :, None]
        folded = weights.reshape(heads_local, G, requests_all, OBS, block_len).sum(axis=(0, 1, 3))
        return (unused, folded)

    _, folded = lax.scan(weight_step, jnp.zeros((), jnp.float32), starts)
    attended = jnp.transpose(folded, (1, 0, 2)).reshape(requests_all, ctx_len)
    rim_width = POOL // 2
    rimmed = extended(attended, (("ctx", 1),), rim_width)
    attended = window_sum(rimmed, ctx_len)
    summed = lax.psum_scatter(attended, "head", scatter_dimension=1, tiled=True)
    total_tokens = ctx_len * lax.axis_size("ctx")
    token_scores = summed * (total_tokens / (OBS * QH * POOL))
    my_index = lax.axis_index("ctx")
    owners = lax.axis_size("ctx")
    pages_here = ctx_len // PAGE
    row_width = heads_local * HD
    key_pages = prefix_keys.reshape(pages_here, PAGE, row_width)
    value_pages = prefix_values.reshape(pages_here, PAGE, row_width)
    wanted = kept_pages.reshape(owners * CAP)
    chosen_keys = jnp.take(key_pages, wanted, axis=0).reshape(owners, CAP, PAGE, row_width)
    chosen_values = jnp.take(value_pages, wanted, axis=0).reshape(owners, CAP, PAGE, row_width)
    slot_tokens = jnp.arange(CAP * PAGE, dtype=jnp.int32) // PAGE
    every_query = jnp.take(dec_query, assignment, axis=0).reshape(owners, SLOTS, heads_local, G, HD)
    their_counts = lax.dynamic_index_in_dim(page_counts, my_index, 1, keepdims=False)
    live_slots = (slot_tokens[None, :] < their_counts[:, None])[:, None, None, None, :]
    keys_by = chosen_keys.reshape(owners, CAP * PAGE, heads_local, HD)
    values_by = chosen_values.reshape(owners, CAP * PAGE, heads_local, HD).astype(jnp.float32)
    scores = (
        jnp.einsum("rskgd,rtkd->rskgt", every_query, keys_by, preferred_element_type=jnp.float32)
        * score_scale
    )
    scores = jnp.where(live_slots, scores, masked_low)
    part_max = jnp.max(scores, axis=-1)
    raised = jnp.where(live_slots, jnp.exp(scores - part_max[..., None]), 0.0)
    part_sum = jnp.sum(raised, axis=-1)
    part_acc = jnp.einsum("rskgt,rtkd->rskgd", raised, values_by, precision=lax.Precision.HIGHEST)
    got_max, got_sum, got_acc = (
        lax.all_to_all(part_max, "ctx", split_axis=0, concat_axis=0, tiled=True),
        lax.all_to_all(part_sum, "ctx", split_axis=0, concat_axis=0, tiled=True),
        lax.all_to_all(part_acc, "ctx", split_axis=0, concat_axis=0, tiled=True),
    )
    joint_max = jnp.max(got_max, axis=0)
    factors = jnp.exp(got_max - joint_max[None])
    running = jnp.sum(got_sum * factors, axis=0)
    attended_values = jnp.sum(got_acc * factors[..., None], axis=0) / running[..., None]
    decode_out = attended_values.reshape(SLOTS, heads_local * G * HD).astype(jnp.bfloat16)
    return (token_scores, decode_out)


def solution(mesh):
    in_specs = (
        P("ctx", "head"),
        P("ctx", "head"),
        P("ctx", "head"),
        P(None, "head"),
        P(None, "ctx", None),
        P(),
        P(),
    )
    out_specs = (P(None, ("ctx", "head")), P("ctx", "head"))
    return jax.shard_map(local, mesh=mesh, in_specs=in_specs, out_specs=out_specs, check_vma=False)
```

profile of v0, /device:TPU:1, one launch (start us, length us, event | category | flops | bytes accessed | tf_op | source)
XLA Modules:
  0.0 264.9 jit_solution(4588463804717518040)
XLA Ops:
  15.7 6.0 %broadcast_select_fusion.1 = (bf16[32,128,512]{2,1,0:T(8,128)(2,1)}, bf16[32,128,512]{2,1,0:T(8,128)(2,1)}) fusion(bf16[32,128,512]{2,1,0:T(8,128)(2,1)} %gather_fusion.1, pred[32]{0:T(512)(128)(4,1)S(1)} %compare_and_fusion, bf16[32,128,512]{2,1,0:T(8,128)(2,1)} %gather_fusion.2), kind=kLoop, calls=%fused_computation.27 | loop fusion | flops 4194304 | bytes 16777248 | tf_op jit(solution)/shard_map/jit(_take)/select_n | solution.py:117
  21.7 7.0 %reshape.148 = bf16[16,256,4,128]{3,2,1,0:T(4,128)(2,1)} reshape(bf16[32,128,512]{2,1,0:T(8,128)(2,1)} %get-tuple-element.316) | data formatting | bytes 8388608 | tf_op jit(solution)/shard_map/reshape;reshape | solution.py:122
  30.2 4.5 %bitcast_reduce_fusion.1 = (f32[16,4,4,5]{3,1,2,0:T(4,128)}, f32[16,4,256,4,5]{2,4,3,1,0:T(8,128)S(1)}) fusion(pred[16,256]{1,0:T(8,128)(4,1)S(1)} %broadcast_compare_fusion, bf16[16,256,4,128,1]{3,2,1,0,4:T(4,128)(2,1)} %bitcast.89, bf16[16,4,4,5,128]{4,3,2,1,0:T(8,128)(2,1)S(1)} %gather.10, pred[16,4]{1,0:T(8,128)(4,1)S(1)} %broadcast_in_dim.71), kind=kOutput, calls=%fused_computation.29 | convolution fusion | flops 85031680 | bytes 5841984 | tf_op jit(solution)/shard_map/rskgd,rtkd->rskgt/dot_general | solution.py:125
  38.7 7.4 %all-to-all-start.2 = ((f32[16,4,4,5]{3,1,2,0:T(4,128)}), f32[16,4,4,5]{3,1,2,0:T(4,128)S(1)}, u32[]{:S(2)}, u32[]{:S(2)}) async-start(f32[16,4,4,5]{3,1,2,0:T(4,128)} %fusion.16), calls=%async_computation.2 | async-start | bytes 262144 | tf_op jit(solution)/shard_map/all_to_all | solution.py:135
  46.1 6.9 %reshape.147 = bf16[16,256,4,128]{3,2,1,0:T(4,128)(2,1)} reshape(bf16[32,128,512]{2,1,0:T(8,128)(2,1)} %get-tuple-element.315) | data formatting | bytes 8388608 | tf_op jit(solution)/shard_map/reshape;reshape | solution.py:123
  53.7 6.3 %all-to-all-start.1 = ((f32[16,4,4,5]{3,1,2,0:T(4,128)}), f32[16,4,4,5]{3,1,2,0:T(4,128)S(1)}, u32[]{:S(2)}, u32[]{:S(2)}) async-start(f32[16,4,4,5]{3,1,2,0:T(4,128)} %get-tuple-element.317), calls=%async_computation.1 | async-start | bytes 262144 | tf_op jit(solution)/shard_map/all_to_all | solution.py:134
  60.0 5.4 %fusion.18 = f32[16,4,4,5,128]{4,3,1,2,0:T(8,128)S(1)} fusion(f32[16,4,256,4,5]{2,4,3,1,0:T(8,128)} %copy-done.3, bf16[16,256,4,128,1]{3,2,1,0,4:T(4,128)(2,1)} %bitcast.90, f32[16,4,4,5]{3,1,2,0:T(4,128)} %get-tuple-element.317, pred[16,256]{1,0:T(8,128)(4,1)S(1)} %broadcast_compare_fusion), kind=kOutput, calls=%fused_computation.34 | convolution fusion | flops 504627200 | bytes 6169600 | tf_op jit(solution)/shard_map/rskgt,rtkd->rskgd/dot_general | solution.py:132
  67.2 5.9 %all-to-all-start = ((f32[16,4,4,5,128]{4,2,3,1,0:T(4,128)}), f32[16,4,4,5,128]{4,2,3,1,0:T(4,128)}, u32[]{:S(2)}, u32[]{:S(2)}) async-start(f32[16,4,4,5,128]{4,2,3,1,0:T(4,128)} %copy.47), calls=%async_computation | async-start | bytes 1310720 | tf_op jit(solution)/shard_map/all_to_all | solution.py:136
  77.9 8.6 %all-to-all-done = f32[16,4,4,5,128]{4,2,3,1,0:T(4,128)} async-done(((f32[16,4,4,5,128]{4,2,3,1,0:T(4,128)}), f32[16,4,4,5,128]{4,2,3,1,0:T(4,128)}, u32[]{:S(2)}, u32[]{:S(2)}) %all-to-all-start) | async-done | bytes 655392 | tf_op jit(solution)/shard_map/all_to_all | solution.py:136
  92.2 28.1 %while.42 = (s32[]{:T(128)}, f32[4,1280]{1,0:T(4,128)S(1)}, f32[4,1280]{1,0:T(4,128)S(1)}, s32[2]{0:T(128)S(1)}, bf16[1024,4,128]{2,0,1:T(8,128)(2,1)S(1)}, /*in...) while((s32[]{:T(128)}, f32[4,1280]{1,0:T(4,128)S(1)}, ...), condition=%wide.region_3.4_spmd.clone, body=%wide.region_0.3_spmd.clone.sunk | while | flops 684221440 | bytes 23072928 | solution.py:92
  95.0 5.5 %bitcast_reduce_fusion.3 = (f32[4,1280]{1,0:T(4,128)S(1)}, f32[4,512,1280]{2,1,0:T(8,128)}) fusion(bf16[4,1280,128]{2,1,0:T(8,128)(2,1)S(1)} %get-tuple-element.461, bf16[1024,4,128]{2,0,1:T(8,128)(2,1)S(1)} %get-tuple-element.460, s32[]{:T(128)S(6)} %select_n.107), kind=kOutput, calls=%fused_computation.13.clone.1 | convolution fusion | flops 676326400 | bytes 12341252 | tf_op jit(solution)/shard_map/while/body/eval_jaxpr/hqd,thd->hqt/dot_general | solution.py:77
  100.5 5.7 %fusion.57 = f32[4,1280]{1,0:T(4,128)S(1)} fusion(f32[4,512,1280]{2,1,0:T(8,128)} %get-tuple-element.437, f32[4,1280]{1,0:T(4,128)S(1)} %select_maximum_fusion.2), kind=kLoop, calls=%fused_computation.15.clone.1 | loop fusion | flops 7859200 | bytes 10526720 | tf_op jit(solution)/shard_map/while/body/eval_jaxpr/reduce_sum | solution.py:85
  109.0 5.5 %bitcast_reduce_fusion.3 = (f32[4,1280]{1,0:T(4,128)S(1)}, f32[4,512,1280]{2,1,0:T(8,128)}) fusion(bf16[4,1280,128]{2,1,0:T(8,128)(2,1)S(1)} %get-tuple-element.461, bf16[1024,4,128]{2,0,1:T(8,128)(2,1)S(1)} %get-tuple-element.460, s32[]{:T(128)S(6)} %select_n.107), kind=kOutput, calls=%fused_computation.13.clone.1 | convolution fusion | flops 676326400 | bytes 12341252 | tf_op jit(solution)/shard_map/while/body/eval_jaxpr/hqd,thd->hqt/dot_general | solution.py:77
  114.6 5.7 %fusion.57 = f32[4,1280]{1,0:T(4,128)S(1)} fusion(f32[4,512,1280]{2,1,0:T(8,128)} %get-tuple-element.437, f32[4,1280]{1,0:T(4,128)S(1)} %select_maximum_fusion.2), kind=kLoop, calls=%fused_computation.15.clone.1 | loop fusion | flops 7859200 | bytes 10526720 | tf_op jit(solution)/shard_map/while/body/eval_jaxpr/reduce_sum | solution.py:85
  120.4 36.9 %all-gather.2 = f32[16,4,1280]{2,1,0:T(4,128)S(1)} all-gather(f32[1,4,1280]{2,1,0:T(4,128)S(1)} %bitcast.92), channel_id=2, replica_groups=mesh['ctx'=16,'head'=2] {'ctx'}, dimensions={0}, use_global_device_ids=true | all-gather | bytes 348160 | tf_op jit(solution)/shard_map/all_gather | solution.py:22
  157.3 30.3 %all-gather.3 = f32[16,4,1280]{2,1,0:T(4,128)S(1)} all-gather(f32[1,4,1280]{2,1,0:T(4,128)S(1)} %bitcast.94), channel_id=3, replica_groups=mesh['ctx'=16,'head'=2] {'ctx'}, dimensions={0}, use_global_device_ids=true | all-gather | bytes 348160 | tf_op jit(solution)/shard_map/all_gather | solution.py:22
  188.3 12.0 %while.40 = (s32[]{:T(128)}, f32[4,1280]{1,0:T(4,128)S(1)}, f32[4,1280]{1,0:T(4,128)S(1)}, f32[16,4,1280]{2,1,0:T(4,128)}, f32[16,4,1280]{2,1,0:T(4,128)}, /*index=5*/s32[]{:T(128)}, s32[]{:T(128)}, s32[]{:T(128)}) while((s32[]{:T(128)}, f32[4,1280]{1,0:T(4,128)S(1)}, f32[4,1280]{1,0:T(4,128)S(1)}, f32[16,4,1280]{2,1,0:T(4,128)}, ...), condition=%wide.region_5.6_spmd, body=%wide.region_4.5_spmd.sunk | while | flops 30725 | bytes 123011 | solution.py:27
  200.3 24.1 %while.41 = (s32[]{:T(128)}, f32[2,4,512]{2,1,0:T(4,128)S(1)}, s32[2]{0:T(128)S(1)}, bf16[1024,4,128]{2,0,1:T(8,128)(2,1)S(1)}, bf16[4,1280,128]{2,1,0:T(8,128)(...) while((s32[]{:T(128)}, f32[2,4,512]{2,1,0:T(4,128)S(1)}, ...), condition=%wide.region_9.10_spmd, body=%wide.region_6.9_spmd.sunk | while | flops 681572352 | bytes 12386479 | solution.py:101
  202.8 4.3 %divide_reduce_fusion.2 = f32[512,1280]{1,0:T(8,128)} fusion(bf16[4,1280,128]{2,1,0:T(8,128)(2,1)S(1)} %get-tuple-element.515, f32[4,1280]{1,0:T(4,128)S(1)} %get-tuple-element.517, f32[4,1280]{1,0:T(4,128)S(1)} %get-tuple-element.516, bf16[1024,4,128]{2,0,1:T(8,128)(2,1)S(1)} %get-tuple-element.514, s32[]{:T(128)S(6)} %select_n.106), kind=kOutput, calls=%fused_computation.8.clone.1 | convolution fusion | flops 680919040 | bytes 4497412 | tf_op jit(solution)/shard_map/while/body/eval_jaxpr/hqd,thd->hqt/dot_general | solution.py:77
  207.1 3.3 %copy.80 = f32[1280,512]{1,0:T(8,128)} copy(f32[1280,512]{0,1:T(8,128)} %bitcast.86) | data formatting | bytes 5242880 | tf_op jit(solution)/shard_map/while/body/eval_jaxpr/reduce_sum | solution.py:98
  214.9 4.3 %divide_reduce_fusion.2 = f32[512,1280]{1,0:T(8,128)} fusion(bf16[4,1280,128]{2,1,0:T(8,128)(2,1)S(1)} %get-tuple-element.515, f32[4,1280]{1,0:T(4,128)S(1)} %get-tuple-element.517, f32[4,1280]{1,0:T(4,128)S(1)} %get-tuple-element.516, bf16[1024,4,128]{2,0,1:T(8,128)(2,1)S(1)} %get-tuple-element.514, s32[]{:T(128)S(6)} %select_n.106), kind=kOutput, calls=%fused_computation.8.clone.1 | convolution fusion | flops 680919040 | bytes 4497412 | tf_op jit(solution)/shard_map/while/body/eval_jaxpr/hqd,thd->hqt/dot_general | solution.py:77
  219.1 3.3 %copy.80 = f32[1280,512]{1,0:T(8,128)} copy(f32[1280,512]{0,1:T(8,128)} %bitcast.86) | data formatting | bytes 5242880 | tf_op jit(solution)/shard_map/while/body/eval_jaxpr/reduce_sum | solution.py:98
  225.7 4.0 %collective-permute-start = (f32[4,3]{1,0:T(4,128)S(1)}, f32[4,3]{1,0:T(4,128)S(1)}, u32[]{:S(2)}, u32[]{:S(2)}) collective-permute-start(f32[4,3]{1,0:T(4,128)S(1)} %get-tuple-element.313), channel_id=1, source_target_pairs={{0,2},{2,4},{4,6},{6,8},{8,10},{10,12},{12,14},{14,16},{16,18},{18... | collective-permute-start | bytes 152 | tf_op jit(solution)/shard_map/ppermute | solution.py:39
  232.4 24.0 %reduce-scatter.4.cloned.1.call-done = f32[512,4]{1,0:T(8,128)} async-done(((f32[1024,4]{1,0:T(8,128)}), f32[512,4]{1,0:T(8,128)}) %reduce-scatter.4.cloned.1.call-update) | async-done | bytes 8208
  (95 shorter events, 51.5 us)
Async XLA Ops:
  7.2 3.0 %copy-start = (bf16[1024,512]{1,0:T(8,128)(2,1)S(1)}, bf16[1024,512]{1,0:T(8,128)(2,1)}, u32[]{:S(2)}) copy-start(bf16[1024,512]{1,0:T(8,128)(2,1)} %param.17) | copy-start | bytes 3145732
  7.2 80.8 %all-gather.6.cloned.1.call-start = ((), (), s32[]{:S(2)}) async-start(), calls=%async_computation.4 | async-start | bytes 1392640 | tf_op jit(solution)/shard_map/all_gather | solution.py:64
  10.1 2.8 %copy-start.1 = (bf16[1024,512]{1,0:T(8,128)(2,1)S(1)}, bf16[1024,512]{1,0:T(8,128)(2,1)}, u32[]{:S(2)}) copy-start(bf16[1024,512]{1,0:T(8,128)(2,1)} %param.16) | copy-start | bytes 3145732
  21.7 7.0 %copy-start.2 = (bf16[64,2560]{1,0:T(8,128)(2,1)S(1)}, bf16[64,2560]{1,0:T(8,128)(2,1)}, u32[]{:S(2)}) copy-start(bf16[64,2560]{1,0:T(8,128)(2,1)} %param.18) | copy-start | bytes 983044
  21.7 8.2 %copy-start.7 = (s32[16,16]{1,0:T(8,128)S(1)}, s32[16,16]{1,0:T(8,128)}, u32[]{:S(2)}) copy-start(s32[16,16]{1,0:T(8,128)} %param.20) | copy-start | bytes 3076
  34.7 1.4 copy-start.3
  38.7 14.4 %all-to-all-start.2 = ((f32[16,4,4,5]{3,1,2,0:T(4,128)}), f32[16,4,4,5]{3,1,2,0:T(4,128)S(1)}, u32[]{:S(2)}, u32[]{:S(2)}) async-start(f32[16,4,4,5]{3,1,2,0:T(4,128)} %fusion.16), calls=%async_computation.2 | async-start | bytes 262144 | tf_op jit(solution)/shard_map/all_to_all | solution.py:135
  53.0 0.7 copy-start.6
  53.7 13.5 %all-to-all-start.1 = ((f32[16,4,4,5]{3,1,2,0:T(4,128)}), f32[16,4,4,5]{3,1,2,0:T(4,128)S(1)}, u32[]{:S(2)}, u32[]{:S(2)}) async-start(f32[16,4,4,5]{3,1,2,0:T(4,128)} %get-tuple-element.317), calls=%async_computation.1 | async-start | bytes 262144 | tf_op jit(solution)/shard_map/all_to_all | solution.py:134
  67.2 19.3 %all-to-all-start = ((f32[16,4,4,5,128]{4,2,3,1,0:T(4,128)}), f32[16,4,4,5,128]{4,2,3,1,0:T(4,128)}, u32[]{:S(2)}, u32[]{:S(2)}) async-start(f32[16,4,4,5,128]{4,2,3,1,0:T(4,128)} %copy.47), calls=%async_computation | async-start | bytes 1310720 | tf_op jit(solution)/shard_map/all_to_all | solution.py:136
  73.1 183.3 %reduce-scatter.4.cloned.1.call-start = ((), (), s32[]{:S(2)}) async-start(), calls=%async_computation.5 | async-start | bytes 786432
  157.2 30.3 %copy-start.4 = (f32[16,4,1280]{2,1,0:T(4,128)}, f32[16,4,1280]{2,1,0:T(4,128)S(1)}, u32[]{:S(2)}) copy-start(f32[16,4,1280]{2,1,0:T(4,128)S(1)} %all-gather.2) | copy-start | bytes 983044
  187.6 0.7 copy-start.5
  224.4 5.3 %collective-permute-start.1 = (f32[4,3]{1,0:T(4,128)S(1)}, f32[4,3]{1,0:T(4,128)S(1)}, u32[]{:S(2)}, u32[]{:S(2)}) collective-permute-start(f32[4,3]{1,0:T(4,128)S(1)} %get-tuple-element.314), channel_id=1, source_target_pairs={{2,0},{4,2},{6,4},{8,6},{10,8},{12,10},{14,12},{16,14},{18,16},{20... | collective-permute-start | bytes 152 | tf_op jit(solution)/shard_map/ppermute | solution.py:40
  225.7 4.8 %collective-permute-start = (f32[4,3]{1,0:T(4,128)S(1)}, f32[4,3]{1,0:T(4,128)S(1)}, u32[]{:S(2)}, u32[]{:S(2)}) collective-permute-start(f32[4,3]{1,0:T(4,128)S(1)} %get-tuple-element.313), channel_id=1, source_target_pairs={{0,2},{2,4},{4,6},{6,8},{8,10},{10,12},{12,14},{14,16},{16,18},{18... | collective-permute-start | bytes 152 | tf_op jit(solution)/shard_map/ppermute | solution.py:39
Sparse Core Ops, SparseCore 0:
  10.8 59.3 all-gather.5
  231.8 24.5 reduce-scatter.3
where the time goes:
time: 267 us; the launch traced here: 265 us
  blocking collectives  67.2 us (25%)
  local copies, waits for them, and re-layouts  45.3 us (17%)
  other arithmetic  40.5 us (15%)
  waiting for transfers between devices  34.5 us (13%)
  matrix products  29.5 us (11%)
  starting transfers between devices  25.3 us (9%)
  between operations  14.3 us (5%)
  loops' own time  8.35 us (3%)
    all_gather x2, blocking collectives, combined_all(): gathered = jax.tree.map(lambda a: lax.all_gather(a, axis), part)  67.2 us
    unnamed x3, waiting for transfers between devices  24.7 us
    dot_general x4, matrix products, block_scores(): jnp.einsum('hqd,thd->hqt', queries, key_block, preferred_element_type=jnp...  19.6 us
    add x15, other arithmetic, merge_stats(): former[1] * jnp.exp(former[0] - joint_max)  11.8 us
    reduce_sum x2, other arithmetic, stats_step(): jnp.sum(jnp.exp(scores - new_max[:, :, None]), axis=2)  11.4 us
    all_to_all x1, waiting for transfers between devices, local(): lax.all_to_all(part_acc, 'ctx', split_axis=0, concat_axis=0, tiled=True)  8.61 us
    all_to_all x1, starting transfers between devices, local(): lax.all_to_all(part_sum, 'ctx', split_axis=0, concat_axis=0, tiled=True)  7.42 us
    another operation x1, local copies, waits for them, and re-layouts, local(): keys_by = chosen_keys.reshape(owners, CAP * PAGE, heads_local, HD)  6.98 us
  transfers between devices with their start and end apart: 7, of which 4 were waited for; matrix products, arithmetic and copies ran while one was open for 19% of the time, Pallas kernels for 0%

commit v1 on v0

v1 whole, which is shorter than its diff:
```python
import functools
import math

import jax
import jax.numpy as jnp
from jax import lax
from jax.experimental import pallas as pl
from jax.experimental.pallas import tpu as pltpu
from jax.sharding import PartitionSpec as P

QH = 40
HD = 128
OBS = 64
POOL = 7
PAGE = 128
SLOTS = 4
G = 5
R = 4
LANES = 128

masked_low = -1e30
MESH = pl.DeviceIdType.MESH
NT = (((1,), (1,)), ((), ()))


def nt_dot(a, b):
    return lax.dot_general(a, b, NT, preferred_element_type=jnp.float32)


def split(x):
    hi = x.astype(jnp.bfloat16)
    return hi, (x - hi.astype(jnp.float32)).astype(jnp.bfloat16)


def kernel(
    n, heads, side, rows,
    obs, keys, values, dec_query, aux,
    tok, dec,
    gath, raised, total, qd, dsend, drecv, stat, srecv, fin, weight, wsend, wrecv, esend, erecv,
    o_send, o_recv, d_send, d_recv, s_send, s_recv, f_send, f_recv, w_send, w_recv, e_send, e_recv,
):
    ctx_len = keys.shape[0]
    kv = keys.shape[1] // HD
    hl = kv * G
    reqs = dec_query.shape[0]
    q_rows = n * rows
    padded_rows = obs.shape[0]
    halves = q_rows // LANES
    chunk_rows = stat.shape[1] // 2
    scale = 1.0 / math.sqrt(HD)
    scale2 = scale * math.log2(math.e)
    me = lax.axis_index("ctx")
    core = lax.axis_index("head")
    major, minor = me // side, me % side
    last = n - 1

    barrier = pltpu.get_barrier_semaphore()

    def greet(who):
        pl.semaphore_signal(barrier, inc=1, device_id=who, device_id_type=MESH)

    @pl.loop(1, n)
    def _(d):
        greet((lax.rem(me + d, n), core))

    for d in range(1, heads):
        other = lax.rem(core + d, heads)
        greet((me, other))

        @pl.when(me > 0)
        def _():
            greet((me - 1, other))

        @pl.when(me < last)
        def _():
            greet((me + 1, other))

    near = jnp.where(me > 0, 1, 0) + jnp.where(me < last, 1, 0)
    pl.semaphore_wait(barrier, n - 1 + (heads - 1) * (1 + near))

    def obs_copy(source, slot, to, sem):
        return pltpu.make_async_remote_copy(
            src_ref=source, dst_ref=gath.at[slot], send_sem=o_send.at[sem],
            recv_sem=o_recv.at[slot], device_id=(to, core), device_id_type=MESH,
        )

    def column(d):
        return lax.rem(major + d, side) * side + minor

    def across(d):
        return major * side + lax.rem(minor + d, side)

    for d in range(1, side):
        obs_copy(obs, me, column(d), d).start()
    for d in range(1, side):
        obs_copy(obs, me, across(d), d * side).start()
    gath[me] = obs[...]

    pick = jnp.where(
        aux[:, 0:1] == lax.broadcasted_iota(jnp.int32, (reqs, reqs), 1), 1.0, 0.0
    ).astype(jnp.bfloat16)
    for k in range(kv):
        cols = pl.ds(k * G * HD, G * HD)
        qd[:, cols] = jnp.dot(
            pick, dec_query[:, cols], preferred_element_type=jnp.float32
        ).astype(jnp.bfloat16)
    page = lax.broadcasted_iota(jnp.int32, (reqs, ctx_len), 1) // PAGE
    bias = jnp.where((page == aux[:, 1:2]) | (page == aux[:, 2:3]), 0.0, masked_low)
    bias = jnp.concatenate([bias] * G, axis=0)
    lane = lax.broadcasted_iota(jnp.int32, (reqs, LANES), 1)

    maxima = jnp.zeros((reqs, LANES), jnp.float32)
    sums = jnp.zeros((reqs, LANES), jnp.float32)
    for k in range(kv):
        q = jnp.concatenate([qd[:, pl.ds((k * G + g) * HD, HD)] for g in range(G)], axis=0)
        s = nt_dot(q, keys[:, pl.ds(k * HD, HD)]) * scale + bias
        top = jnp.max(s, axis=1, keepdims=True)
        e = jnp.exp(s - top)
        amount = jnp.sum(e, axis=1, keepdims=True)
        hi, lo = split(e)
        v = values[:, pl.ds(k * HD, HD)]
        acc = jnp.dot(hi, v, preferred_element_type=jnp.float32) + jnp.dot(
            lo, v, preferred_element_type=jnp.float32
        )
        for g in range(G):
            h = k * G + g
            part = slice(g * reqs, (g + 1) * reqs)
            maxima = jnp.where(lane == h, top[part], maxima)
            sums = jnp.where(lane == h, amount[part], sums)
            for p in range(n):
                at = g * reqs + p * SLOTS
                dsend[p, h] = acc[at : at + SLOTS]
        if k == 0:
            for d in range(1, side):
                slot = column(d)
                obs_copy(obs, slot, me, d).wait_recv()
                for f in range(1, side):
                    obs_copy(gath.at[slot], slot, across(f), f * side + d).start()
    for p in range(n):
        dsend[p, hl] = maxima[p * SLOTS : (p + 1) * SLOTS]
        dsend[p, hl + 1] = sums[p * SLOTS : (p + 1) * SLOTS]

    def spread(source, target, send, recv):
        def copy(d):
            to = lax.rem(me + d, n)
            return pltpu.make_async_remote_copy(
                src_ref=source(to), dst_ref=target.at[me], send_sem=send.at[d],
                recv_sem=recv.at[me], device_id=(to, core), device_id_type=MESH,
            )

        def arrival(d):
            frm = lax.rem(me + n - d, n)
            return pltpu.make_async_remote_copy(
                src_ref=source(frm), dst_ref=target.at[frm], send_sem=send.at[d],
                recv_sem=recv.at[frm], device_id=(frm, core), device_id_type=MESH,
            )

        def start():
            @pl.loop(1, n)
            def _(d):
                copy(d).start()

        def finish():
            @pl.loop(1, n)
            def _(d):
                arrival(d).wait_recv()

        def drain():
            @pl.loop(1, n)
            def _(d):
                copy(d).wait_send()

        return start, finish, drain

    d_start, d_finish, d_drain = spread(lambda to: dsend.at[to], drecv, d_send, d_recv)
    s_start, s_finish, s_drain = spread(lambda to: stat.at[to], srecv, s_send, s_recv)
    f_start, f_finish, f_drain = spread(lambda to: fin.at[me], fin, f_send, f_recv)
    d_start()
    drecv[me] = dsend[me]

    for f in range(1, side):
        for d in range(side):
            slot = lax.rem(major + d, side) * side + lax.rem(minor + f, side)
            obs_copy(obs, slot, me, d).wait_recv()

    stat[...] = jnp.zeros_like(stat)

    @pl.loop(0, hl)
    def _(h):
        cols = pl.ds(pl.multiple_of(h * HD, HD), HD)
        q = gath[:, :, cols].reshape(n * padded_rows, HD)
        if padded_rows != rows:
            shape = (q_rows, n * padded_rows)
            row = lax.broadcasted_iota(jnp.int32, shape, 0)
            col = lax.broadcasted_iota(jnp.int32, shape, 1)
            keep = (row // rows) * padded_rows + row % rows == col
            q = jnp.dot(
                jnp.where(keep, 1.0, 0.0).astype(jnp.bfloat16), q,
                preferred_element_type=jnp.float32,
            ).astype(jnp.bfloat16)
        s = nt_dot(keys[:, pl.ds(pl.multiple_of((h // G) * HD, HD), HD)], q)
        top = jnp.max(s, axis=0, keepdims=True)
        e = jnp.exp2((s - top) * scale2)
        raised[h] = e
        amount = jnp.sum(e, axis=0, keepdims=True)
        for half in range(halves):
            at = h * halves + half
            part = slice(half * LANES, (half + 1) * LANES)
            stat[at // chunk_rows, pl.ds(at % chunk_rows, 1), :] = top[:, part]
            stat[at // chunk_rows, pl.ds(chunk_rows + at % chunk_rows, 1), :] = amount[:, part]

    s_start()
    srecv[me] = stat[me]
    s_finish()
    tops = [srecv[i, 0:chunk_rows, :] for i in range(n)]
    joint = functools.reduce(jnp.maximum, tops)
    gross = jnp.zeros_like(joint)
    for i in range(n):
        gross = gross + srecv[i, chunk_rows : 2 * chunk_rows, :] * jnp.exp2(
            (tops[i] - joint) * scale2
        )
    fin[me] = jnp.concatenate([joint, gross], axis=0)
    f_start()

    d_finish()
    joint_max = drecv[0, hl]
    for i in range(1, n):
        joint_max = jnp.maximum(joint_max, drecv[i, hl])
    factors = [jnp.exp(drecv[i, hl] - joint_max) for i in range(n)]
    running = factors[0] * drecv[0, hl + 1]
    for i in range(1, n):
        running = running + factors[i] * drecv[i, hl + 1]
    inverse = 1.0 / running
    factors = [f * inverse for f in factors]
    for h in range(hl):
        out = factors[0][:, h : h + 1] * drecv[0, h]
        for i in range(1, n):
            out = out + factors[i][:, h : h + 1] * drecv[i, h]
        dec[:, pl.ds(h * HD, HD)] = out.astype(jnp.bfloat16)

    f_finish()

    @pl.loop(0, hl)
    def _(h):
        for half in range(halves):
            at = h * halves + half
            own, low = at // chunk_rows, at % chunk_rows
            mine = stat[own, pl.ds(low, 1), :]
            whole = fin[own, pl.ds(low, 1), :]
            amount = fin[own, pl.ds(chunk_rows + low, 1), :]
            weight[h, :, pl.ds(half * LANES, LANES)] = jnp.exp2((mine - whole) * scale2) / amount

    block = 64

    @pl.loop(0, ctx_len // block)
    def _(b):
        at = pl.ds(pl.multiple_of(b * block, block), block)

        def add(h, acc):
            return acc + raised[h, at, :] * weight[h]

        total[at, :] = lax.fori_loop(
            0, hl, add, jnp.zeros((block, q_rows), jnp.float32), unroll=True
        )

    request = lax.broadcasted_iota(jnp.int32, (8, q_rows), 1) // OBS
    fold = jnp.where(request == lax.broadcasted_iota(jnp.int32, (8, q_rows), 0), 1.0, 0.0)
    fold = fold.astype(jnp.bfloat16)
    hi, lo = split(total[...])
    attended = nt_dot(fold, hi) + nt_dot(fold, lo)
    zeros = jnp.zeros((8, LANES), jnp.float32)
    wide = jnp.concatenate([zeros, attended, zeros], axis=1)
    width = ctx_len + 2 * LANES
    pooled = wide
    for d in range(1, POOL // 2 + 1):
        pooled = pooled + pltpu.roll(wide, d, 1) + pltpu.roll(wide, width - d, 1)
    pooled = pooled * (ctx_len * n / (OBS * QH * POOL))
    span = ctx_len // heads
    for j in range(heads):
        wsend[j] = pooled[:, LANES + j * span : LANES + (j + 1) * span]
    esend[0] = pooled[:, :LANES]
    esend[1] = pooled[:, LANES + ctx_len :]

    def w_copy(d, to):
        return pltpu.make_async_remote_copy(
            src_ref=wsend.at[to], dst_ref=wrecv.at[core], send_sem=w_send.at[d],
            recv_sem=w_recv.at[core], device_id=(me, to), device_id_type=MESH,
        )

    def w_arrival(frm):
        return pltpu.make_async_remote_copy(
            src_ref=wsend.at[frm], dst_ref=wrecv.at[frm], send_sem=w_send.at[0],
            recv_sem=w_recv.at[frm], device_id=(me, frm), device_id_type=MESH,
        )

    def e_copy(side_of, to_ctx, to_core, slot):
        return pltpu.make_async_remote_copy(
            src_ref=esend.at[side_of], dst_ref=erecv.at[slot], send_sem=e_send.at[side_of],
            recv_sem=e_recv.at[slot], device_id=(to_ctx, to_core), device_id_type=MESH,
        )

    @pl.when(me > 0)
    def _():
        e_copy(0, me - 1, heads - 1, core).start()

    @pl.when(me < last)
    def _():
        e_copy(1, me + 1, 0, core).start()

    for d in range(1, heads):
        w_copy(d, lax.rem(core + d, heads)).start()
    wrecv[core] = wsend[core]
    for d in range(1, heads):
        w_arrival(lax.rem(core + d, heads)).wait_recv()
    result = wrecv[0]
    for j in range(1, heads):
        result = result + wrecv[j]
    tok[...] = result[:R]

    def edge():
        for j in range(heads):
            e_copy(0, me, core, j).wait_recv()
        rim = erecv[0]
        for j in range(1, heads):
            rim = rim + erecv[j]
        return rim[:R]

    @pl.when((core == 0) & (me > 0))
    def _():
        tok[:, 0:LANES] = tok[:, 0:LANES] + edge()

    @pl.when((core == heads - 1) & (me < last))
    def _():
        tok[:, span - LANES : span] = tok[:, span - LANES : span] + edge()

    for d in range(1, side):
        obs_copy(obs, me, column(d), d).wait_send()
        obs_copy(obs, me, across(d), d * side).wait_send()
        for f in range(1, side):
            slot = column(d)
            obs_copy(gath.at[slot], slot, across(f), f * side + d).wait_send()
    d_drain()
    s_drain()
    f_drain()
    for d in range(1, heads):
        w_copy(d, lax.rem(core + d, heads)).wait_send()

    @pl.when(me > 0)
    def _():
        e_copy(0, me - 1, heads - 1, core).wait_send()

    @pl.when(me < last)
    def _():
        e_copy(1, me + 1, 0, core).wait_send()


def local(n, heads, obs_query, prefix_keys, prefix_values, dec_query, kept_pages, page_counts, assignment):
    rows, width = obs_query.shape
    ctx_len = prefix_keys.shape[0]
    hl = width // HD
    reqs = dec_query.shape[0]
    q_rows = n * rows
    side = math.isqrt(n)
    while n % side:
        side -= 1
    padded_rows = -(-rows // 16) * 16
    obs = jnp.pad(obs_query, ((0, padded_rows - rows), (0, 0)))
    counts = lax.dynamic_index_in_dim(page_counts, lax.axis_index("ctx"), 1, keepdims=True)
    cap = kept_pages.shape[2]
    live = jnp.arange(cap, dtype=jnp.int32)[None, :] < counts
    kept = jnp.where(live, kept_pages[:, 0, :], -1)
    aux = jnp.concatenate([assignment[:, None], jnp.repeat(kept, SLOTS, axis=0)], axis=1)
    chunk_rows = -(-(hl * q_rows // LANES) // n)
    f32 = jnp.float32
    span = ctx_len // heads
    dma = pltpu.SemaphoreType.DMA
    vmem = pl.BlockSpec(memory_space=pltpu.VMEM)
    return pl.pallas_call(
        functools.partial(kernel, n, heads, side, rows),
        out_shape=(
            jax.ShapeDtypeStruct((R, span), f32),
            jax.ShapeDtypeStruct((SLOTS, width), jnp.bfloat16),
        ),
        in_specs=[vmem] * 5,
        out_specs=(vmem, vmem),
        scratch_shapes=[
            pltpu.VMEM((n, padded_rows, width), jnp.bfloat16),
            pltpu.VMEM((hl, ctx_len, q_rows), f32),
            pltpu.VMEM((ctx_len, q_rows), f32),
            pltpu.VMEM((reqs, width), jnp.bfloat16),
            pltpu.VMEM((n, hl + 2, SLOTS, LANES), f32),
            pltpu.VMEM((n, hl + 2, SLOTS, LANES), f32),
            pltpu.VMEM((n, 2 * chunk_rows, LANES), f32),
            pltpu.VMEM((n, 2 * chunk_rows, LANES), f32),
            pltpu.VMEM((n, 2 * chunk_rows, LANES), f32),
            pltpu.VMEM((hl, 1, q_rows), f32),
            pltpu.VMEM((heads, 8, span), f32),
            pltpu.VMEM((heads, 8, span), f32),
            pltpu.VMEM((2, 8, LANES), f32),
            pltpu.VMEM((heads, 8, LANES), f32),
            dma((side * side,)), dma((n,)),
            dma((n,)), dma((n,)),
            dma((n,)), dma((n,)),
            dma((n,)), dma((n,)),
            dma((heads,)), dma((heads,)),
            dma((2,)), dma((heads,)),
        ],
        compiler_params=pltpu.CompilerParams(
            collective_id=0, has_side_effects=True, vmem_limit_bytes=50 * 1024 * 1024
        ),
        cost_estimate=pl.CostEstimate(
            flops=4 * hl * q_rows * ctx_len * HD, bytes_accessed=4 * ctx_len * width,
            transcendentals=hl * q_rows * ctx_len,
        ),
    )(obs, prefix_keys, prefix_values, dec_query, aux)


def solution(mesh):
    in_specs = (
        P("ctx", "head"),
        P("ctx", "head"),
        P("ctx", "head"),
        P(None, "head"),
        P(None, "ctx", None),
        P(),
        P(),
    )
    out_specs = (P(None, ("ctx", "head")), P("ctx", "head"))
    body = functools.partial(local, mesh.shape["ctx"], mesh.shape["head"])
    return jax.shard_map(body, mesh=mesh, in_specs=in_specs, out_specs=out_specs, check_vma=False)
```

time: 267 us -> 67.4 us (0.25)
  blocking collectives: 67.2 us -> 0 us
  Pallas kernels: 0 us -> 59.4 us
  local copies, waits for them, and re-layouts: 45.3 us -> 5.75 us
  other arithmetic: 40.5 us -> 1.35 us
  waiting for transfers between devices: 34.5 us -> 0 us
  matrix products: 29.5 us -> 0 us
  starting transfers between devices: 25.3 us -> 0 us
  between operations: 14.3 us -> 0.67 us
  loops' own time: 8.35 us -> 0 us
    all_gather x2 -> x0, blocking collectives: 67.2 us -> none  [combined_all(): gathered = jax.tree.map(lambda a: lax.all_gather(a, axis), part)]
    pallas_call x0 -> x1, Pallas kernels: none -> 59.4 us  [local(): pl.pallas_call(functools.partial(kernel, n, heads, side, rows), out_shape...]
    dot_general x6 -> x0, matrix products: 29.5 us -> none  [the longest x4 19.6 us: block_scores(): jnp.einsum('hqd,thd->hqt', queries, key_block, preferred_element_type=jnp...]
    unnamed x3 -> x0, waiting for transfers between devices: 24.7 us -> none
    reduce_sum x7 -> x0, other arithmetic: 20.4 us -> none  [the longest x2 11.4 us: stats_step(): jnp.sum(jnp.exp(scores - new_max[:, :, None]), axis=2)]
    all_to_all x3 -> x0, starting transfers between devices: 19.7 us -> none  [the longest x1 7.42 us: local(): lax.all_to_all(part_sum, 'ctx', split_axis=0, concat_axis=0, tiled=True)]
    another operation x2 -> x0, local copies, waits for them, and re-layouts: 13.9 us -> none  [the longest x1 6.98 us: local(): keys_by = chosen_keys.reshape(owners, CAP * PAGE, heads_local, HD)]
    add x18 -> x0, other arithmetic: 12 us -> none  [the longest x15 11.8 us: merge_stats(): former[1] * jnp.exp(former[0] - joint_max)]
  transfers between devices with their start and end apart: 7 -> 0, of which waited for: 4 -> 0; matrix products, arithmetic and copies ran while one was open for 19% -> 0% of each run, Pallas kernels for 0% -> 0%
where the time goes in v1:
time: 67.4 us; the launch traced here: 67.2 us
  Pallas kernels  59.4 us (88%)
  local copies, waits for them, and re-layouts  5.75 us (9%)
  other arithmetic  1.35 us (2%)
    pallas_call x1, Pallas kernels, local(): pl.pallas_call(functools.partial(kernel, n, heads, side, rows), out_shape...  59.4 us
    unnamed x12, local copies, waits for them, and re-layouts  5.31 us

profile of v1, /device:TPU:1, one launch (start us, length us, event | category | flops | bytes accessed | tf_op | source)
XLA Modules:
  0.0 67.2 jit_solution(10314510879612195067)
XLA Ops:
  0.6 0.0 copy-start
  0.6 0.0 copy-start.4
  0.7 0.7 %copy-done = s32[16,16]{1,0:T(8,128)S(1)} copy-done((s32[16,16]{1,0:T(8,128)S(1)}, s32[16,16]{1,0:T(8,128)}, u32[]{:S(2)}) %copy-start) | copy-done | bytes 1048
  1.3 0.2 dynamic-slice_reduce_fusion
  1.5 0.7 %compare_select_fusion = s32[16,2]{0,1:T(2,128)S(1)} fusion(s32[16,1,2]{0,2,1:T(2,128)} %param.11, s32[16]{0:T(128)S(1)} %dynamic-slice_reduce_fusion), kind=kLoop, calls=%fused_computation.2 | loop fusion | flops 64 | bytes 320 | tf_op jit(solution)/shard_map/jit(_where)/select_n | solution.py:371
  2.2 0.1 broadcast_in_dim.13
  2.3 0.1 reshape.7
  2.4 0.7 pad_add_fusion
  3.0 0.1 copy.13.aux
  3.1 0.0 copy-done.4
  3.1 0.0 copy-start.1
  3.1 1.2 %copy-done.1 = bf16[1024,512]{1,0:T(8,128)(2,1)S(1)} copy-done((bf16[1024,512]{1,0:T(8,128)(2,1)S(1)}, bf16[1024,512]{1,0:T(8,128)(2,1)}, u32[]{:S(2)}) %copy-start.1) | copy-done | bytes 1048600
  4.4 0.0 copy-start.2
  4.4 1.2 %copy-done.2 = bf16[1024,512]{1,0:T(8,128)(2,1)S(1)} copy-done((bf16[1024,512]{1,0:T(8,128)(2,1)S(1)}, bf16[1024,512]{1,0:T(8,128)(2,1)}, u32[]{:S(2)}) %copy-start.2) | copy-done | bytes 1048600
  5.6 0.0 copy-start.3
  5.6 1.0 %copy-done.3 = bf16[64,2560]{1,0:T(8,128)(2,1)S(1)} copy-done((bf16[64,2560]{1,0:T(8,128)(2,1)S(1)}, bf16[64,2560]{1,0:T(8,128)(2,1)}, u32[]{:S(2)}) %copy-start.3) | copy-done | bytes 327704
  6.6 59.4 %shard_map.86 = (f32[4,512]{1,0:T(4,128)S(1)}, bf16[4,2560]{1,0:T(4,128)(2,1)S(1)}) custom-call(bf16[16,2560]{1,0:T(8,128)(2,1)S(1)} %copy-done.4, bf16[1024,512]{1,0:T(8,128)(2,1)S(1)} %copy-done.1, bf16[1024,512]{1,0:T(8,128)(2,1)S(1)} %copy-done.2, bf16[64,2560]{1,0:T(8,128)(2,1)S(1)} %copy-done.3, s32[64,3]{1,0:T(8,128)S(1)} %copy.13.aux), custom_call_target="tpu_custom_call" | custom-call | flops 2684354560 | bytes 10485760 | tf_op jit(solution)/shard_map/pallas_call | solution.py:378
  66.0 0.6 copy.16
  66.6 0.6 copy.17
Async XLA Ops:
  0.6 0.7 %copy-start = (s32[16,16]{1,0:T(8,128)S(1)}, s32[16,16]{1,0:T(8,128)}, u32[]{:S(2)}) copy-start(s32[16,16]{1,0:T(8,128)} %param.12) | copy-start | bytes 3076
  0.6 2.5 %copy-start.4 = (bf16[16,2560]{1,0:T(8,128)(2,1)S(1)}, bf16[16,2560]{1,0:T(8,128)(2,1)}, u32[]{:S(2)}) copy-start(bf16[16,2560]{1,0:T(8,128)(2,1)} %obs.1) | copy-start | bytes 245764
  3.1 1.2 %copy-start.1 = (bf16[1024,512]{1,0:T(8,128)(2,1)S(1)}, bf16[1024,512]{1,0:T(8,128)(2,1)}, u32[]{:S(2)}) copy-start(bf16[1024,512]{1,0:T(8,128)(2,1)} %keys.1) | copy-start | bytes 3145732
  4.4 1.2 %copy-start.2 = (bf16[1024,512]{1,0:T(8,128)(2,1)S(1)}, bf16[1024,512]{1,0:T(8,128)(2,1)}, u32[]{:S(2)}) copy-start(bf16[1024,512]{1,0:T(8,128)(2,1)} %values.1) | copy-start | bytes 3145732
  5.6 1.0 %copy-start.3 = (bf16[64,2560]{1,0:T(8,128)(2,1)S(1)}, bf16[64,2560]{1,0:T(8,128)(2,1)}, u32[]{:S(2)}) copy-start(bf16[64,2560]{1,0:T(8,128)(2,1)} %dec_query.1) | copy-start | bytes 983044

commit v2 on v1

--- a/solution.py
+++ b/solution.py
@@ -17,6 +17,7 @@
 G = 5
 R = 4
 LANES = 128
+EARLY = 0
 
 masked_low = -1e30
 MESH = pl.DeviceIdType.MESH
@@ -34,10 +35,10 @@
 
 def kernel(
     n, heads, side, rows,
-    obs, keys, values, dec_query, aux,
+    obs, keys_in, values_in, dec_query_in, assign, kept, counts,
     tok, dec,
-    gath, raised, total, qd, dsend, drecv, stat, srecv, fin, weight, wsend, wrecv, esend, erecv,
-    o_send, o_recv, d_send, d_recv, s_send, s_recv, f_send, f_recv, w_send, w_recv, e_send, e_recv,
+    keys, values, dec_query, gath, raised, total, qd, dsend, drecv, stat, srecv, fin, weight, wsend, wrecv, esend, erecv,
+    o_send, o_recv, d_send, d_recv, s_send, s_recv, f_send, f_recv, w_send, w_recv, e_send, e_recv, l_sem,
 ):
     ctx_len = keys.shape[0]
     kv = keys.shape[1] // HD
@@ -75,9 +76,15 @@
         def _():
             greet((me + 1, other))
 
+    loads = [
+        pltpu.make_async_copy(dec_query_in, dec_query, l_sem.at[0]),
+        pltpu.make_async_copy(keys_in, keys, l_sem.at[1]),
+        pltpu.make_async_copy(values_in, values, l_sem.at[2]),
+    ]
+    for load in loads:
+        load.start()
+
     near = jnp.where(me > 0, 1, 0) + jnp.where(me < last, 1, 0)
-    pl.semaphore_wait(barrier, n - 1 + (heads - 1) * (1 + near))
-
     def obs_copy(source, slot, to, sem):
         return pltpu.make_async_remote_copy(
             src_ref=source, dst_ref=gath.at[slot], send_sem=o_send.at[sem],
@@ -90,28 +97,58 @@
     def across(d):
         return major * side + lax.rem(minor + d, side)
 
-    for d in range(1, side):
-        obs_copy(obs, me, column(d), d).start()
-    for d in range(1, side):
-        obs_copy(obs, me, across(d), d * side).start()
     gath[me] = obs[...]
-
+    owner = lax.broadcasted_iota(jnp.int32, (reqs, n), 0) // SLOTS
+    source = lax.broadcasted_iota(jnp.int32, (reqs, n), 1)
+    mine = owner == source
+    count = jnp.dot(
+        jnp.where(mine, 1.0, 0.0).astype(jnp.bfloat16),
+        counts[...].astype(jnp.float32).astype(jnp.bfloat16),
+        preferred_element_type=jnp.float32,
+    )
+    count = jnp.sum(jnp.where(source == me, count, 0.0), axis=1, keepdims=True)
+    page = lax.broadcasted_iota(jnp.int32, (reqs, ctx_len), 1) // PAGE
+    page = page.astype(jnp.float32)
+    bias = jnp.full((reqs, ctx_len), masked_low, jnp.float32)
+    for j in range(kept.shape[0]):
+        slot_page = jnp.where(mine, kept[j : j + 1, :].astype(jnp.float32), 0.0)
+        slot_page = jnp.sum(slot_page, axis=1, keepdims=True)
+        slot_page = jnp.where(count > j, slot_page, -1.0)
+        bias = jnp.where(page == slot_page, 0.0, bias)
+    bias = jnp.concatenate([bias] * G, axis=0)
+    lane = lax.broadcasted_iota(jnp.int32, (reqs, LANES), 1)
     pick = jnp.where(
-        aux[:, 0:1] == lax.broadcasted_iota(jnp.int32, (reqs, reqs), 1), 1.0, 0.0
+        assign[...] == lax.broadcasted_iota(jnp.int32, (reqs, reqs), 0), 1.0, 0.0
     ).astype(jnp.bfloat16)
+    loads[0].wait()
     for k in range(kv):
         cols = pl.ds(k * G * HD, G * HD)
-        qd[:, cols] = jnp.dot(
-            pick, dec_query[:, cols], preferred_element_type=jnp.float32
+        qd[:, cols] = lax.dot_general(
+            pick, dec_query[:, cols], (((0,), (0,)), ((), ())),
+            preferred_element_type=jnp.float32,
         ).astype(jnp.bfloat16)
-    page = lax.broadcasted_iota(jnp.int32, (reqs, ctx_len), 1) // PAGE
-    bias = jnp.where((page == aux[:, 1:2]) | (page == aux[:, 2:3]), 0.0, masked_low)
-    bias = jnp.concatenate([bias] * G, axis=0)
-    lane = lax.broadcasted_iota(jnp.int32, (reqs, LANES), 1)
+    loads[1].wait()
+    loads[2].wait()
 
     maxima = jnp.zeros((reqs, LANES), jnp.float32)
     sums = jnp.zeros((reqs, LANES), jnp.float32)
+
+    def forward(m):
+        slot = m * side + minor
+
+        @pl.when(major != m)
+        def _():
+            obs_copy(obs, slot, me, 0).wait_recv()
+
+        for f in range(1, side):
+            obs_copy(gath.at[slot], slot, across(f), f * side + m).start()
+
+    ahead = min(EARLY, kv - 1)
     for k in range(kv):
+        if k == ahead:
+            pl.semaphore_wait(barrier, n - 1 + (heads - 1) * (1 + near))
+            for d in range(1, side):
+                obs_copy(obs, me, column(d), d).start()
         q = jnp.concatenate([qd[:, pl.ds((k * G + g) * HD, HD)] for g in range(G)], axis=0)
         s = nt_dot(q, keys[:, pl.ds(k * HD, HD)]) * scale + bias
         top = jnp.max(s, axis=1, keepdims=True)
@@ -130,12 +167,10 @@
             for p in range(n):
                 at = g * reqs + p * SLOTS
                 dsend[p, h] = acc[at : at + SLOTS]
-        if k == 0:
-            for d in range(1, side):
-                slot = column(d)
-                obs_copy(obs, slot, me, d).wait_recv()
-                for f in range(1, side):
-                    obs_copy(gath.at[slot], slot, across(f), f * side + d).start()
+        if k > ahead:
+            forward(k - ahead - 1)
+    for m in range(kv - ahead - 1, side):
+        forward(m)
     for p in range(n):
         dsend[p, hl] = maxima[p * SLOTS : (p + 1) * SLOTS]
         dsend[p, hl + 1] = sums[p * SLOTS : (p + 1) * SLOTS]
@@ -175,39 +210,42 @@
     d_start, d_finish, d_drain = spread(lambda to: dsend.at[to], drecv, d_send, d_recv)
     s_start, s_finish, s_drain = spread(lambda to: stat.at[to], srecv, s_send, s_recv)
     f_start, f_finish, f_drain = spread(lambda to: fin.at[me], fin, f_send, f_recv)
-    d_start()
     drecv[me] = dsend[me]
-
-    for f in range(1, side):
-        for d in range(side):
-            slot = lax.rem(major + d, side) * side + lax.rem(minor + f, side)
-            obs_copy(obs, slot, me, d).wait_recv()
-
     stat[...] = jnp.zeros_like(stat)
-
-    @pl.loop(0, hl)
-    def _(h):
-        cols = pl.ds(pl.multiple_of(h * HD, HD), HD)
-        q = gath[:, :, cols].reshape(n * padded_rows, HD)
-        if padded_rows != rows:
-            shape = (q_rows, n * padded_rows)
-            row = lax.broadcasted_iota(jnp.int32, shape, 0)
-            col = lax.broadcasted_iota(jnp.int32, shape, 1)
-            keep = (row // rows) * padded_rows + row % rows == col
-            q = jnp.dot(
-                jnp.where(keep, 1.0, 0.0).astype(jnp.bfloat16), q,
-                preferred_element_type=jnp.float32,
-            ).astype(jnp.bfloat16)
-        s = nt_dot(keys[:, pl.ds(pl.multiple_of((h // G) * HD, HD), HD)], q)
-        top = jnp.max(s, axis=0, keepdims=True)
-        e = jnp.exp2((s - top) * scale2)
-        raised[h] = e
-        amount = jnp.sum(e, axis=0, keepdims=True)
-        for half in range(halves):
+    per_half = n // halves
+    majors_half = side // halves
+
+    for half in range(halves):
+        for m in range(half * majors_half, (half + 1) * majors_half):
+            for f in range(1, side):
+                slot = m * side + lax.rem(minor + f, side)
+                obs_copy(obs, slot, me, 0).wait_recv()
+        if half == halves - 1:
+            d_start()
+
+        @pl.loop(0, hl, unroll=2)
+        def _(h):
+            cols = pl.ds(pl.multiple_of(h * HD, HD), HD)
+            q = gath[half * per_half : (half + 1) * per_half, :, cols]
+            q = q.reshape(per_half * padded_rows, HD)
+            if padded_rows != rows:
+                shape = (LANES, per_half * padded_rows)
+                row = lax.broadcasted_iota(jnp.int32, shape, 0)
+                col = lax.broadcasted_iota(jnp.int32, shape, 1)
+                keep = (row // rows) * padded_rows + row % rows == col
+                q = jnp.dot(
+                    jnp.where(keep, 1.0, 0.0).astype(jnp.bfloat16), q,
+                    preferred_element_type=jnp.float32,
+                ).astype(jnp.bfloat16)
+            s = nt_dot(keys[:, pl.ds(pl.multiple_of((h // G) * HD, HD), HD)], q)
+            top = jnp.max(s, axis=0, keepdims=True)
+            e = jnp.exp2((s - top) * scale2)
+            raised[half, h] = e
             at = h * halves + half
-            part = slice(half * LANES, (half + 1) * LANES)
-            stat[at // chunk_rows, pl.ds(at % chunk_rows, 1), :] = top[:, part]
-            stat[at // chunk_rows, pl.ds(chunk_rows + at % chunk_rows, 1), :] = amount[:, part]
+            stat[at // chunk_rows, pl.ds(at % chunk_rows, 1), :] = top
+            stat[at // chunk_rows, pl.ds(chunk_rows + at % chunk_rows, 1), :] = jnp.sum(
+                e, axis=0, keepdims=True
+            )
 
     s_start()
     srecv[me] = stat[me]
@@ -248,20 +286,22 @@
             mine = stat[own, pl.ds(low, 1), :]
             whole = fin[own, pl.ds(low, 1), :]
             amount = fin[own, pl.ds(chunk_rows + low, 1), :]
-            weight[h, :, pl.ds(half * LANES, LANES)] = jnp.exp2((mine - whole) * scale2) / amount
-
-    block = 64
-
-    @pl.loop(0, ctx_len // block)
-    def _(b):
-        at = pl.ds(pl.multiple_of(b * block, block), block)
-
-        def add(h, acc):
-            return acc + raised[h, at, :] * weight[h]
-
-        total[at, :] = lax.fori_loop(
-            0, hl, add, jnp.zeros((block, q_rows), jnp.float32), unroll=True
-        )
+            weight[half, h] = jnp.exp2((mine - whole) * scale2) / amount
+
+    block = 128
+
+    for half in range(halves):
+
+        @pl.loop(0, ctx_len // block)
+        def _(b):
+            at = pl.ds(pl.multiple_of(b * block, block), block)
+
+            def add(h, acc):
+                return acc + raised[half, h, at, :] * weight[half, h]
+
+            total[at, half * LANES : (half + 1) * LANES] = lax.fori_loop(
+                0, hl, add, jnp.zeros((block, LANES), jnp.float32), unroll=True
+            )
 
     request = lax.broadcasted_iota(jnp.int32, (8, q_rows), 1) // OBS
     fold = jnp.where(request == lax.broadcasted_iota(jnp.int32, (8, q_rows), 0), 1.0, 0.0)
@@ -335,10 +375,10 @@
 
     for d in range(1, side):
         obs_copy(obs, me, column(d), d).wait_send()
-        obs_copy(obs, me, across(d), d * side).wait_send()
+    for m in range(side):
         for f in range(1, side):
-            slot = column(d)
-            obs_copy(gath.at[slot], slot, across(f), f * side + d).wait_send()
+            slot = m * side + minor
+            obs_copy(gath.at[slot], slot, across(f), f * side + m).wait_send()
     d_drain()
     s_drain()
     f_drain()
@@ -365,11 +405,8 @@
         side -= 1
     padded_rows = -(-rows // 16) * 16
     obs = jnp.pad(obs_query, ((0, padded_rows - rows), (0, 0)))
-    counts = lax.dynamic_index_in_dim(page_counts, lax.axis_index("ctx"), 1, keepdims=True)
-    cap = kept_pages.shape[2]
-    live = jnp.arange(cap, dtype=jnp.int32)[None, :] < counts
-    kept = jnp.where(live, kept_pages[:, 0, :], -1)
-    aux = jnp.concatenate([assignment[:, None], jnp.repeat(kept, SLOTS, axis=0)], axis=1)
+    kept = jnp.transpose(kept_pages, (1, 2, 0)).reshape(kept_pages.shape[2], n)
+    assign = assignment.reshape(1, reqs)
     chunk_rows = -(-(hl * q_rows // LANES) // n)
     f32 = jnp.float32
     span = ctx_len // heads
@@ -381,11 +418,14 @@
             jax.ShapeDtypeStruct((R, span), f32),
             jax.ShapeDtypeStruct((SLOTS, width), jnp.bfloat16),
         ),
-        in_specs=[vmem] * 5,
+        in_specs=[vmem] + [pl.BlockSpec(memory_space=pl.ANY)] * 3 + [vmem] * 3,
         out_specs=(vmem, vmem),
         scratch_shapes=[
+            pltpu.VMEM(prefix_keys.shape, jnp.bfloat16),
+            pltpu.VMEM(prefix_values.shape, jnp.bfloat16),
+            pltpu.VMEM(dec_query.shape, jnp.bfloat16),
             pltpu.VMEM((n, padded_rows, width), jnp.bfloat16),
-            pltpu.VMEM((hl, ctx_len, q_rows), f32),
+            pltpu.VMEM((q_rows // LANES, hl, ctx_len, LANES), f32),
             pltpu.VMEM((ctx_len, q_rows), f32),
             pltpu.VMEM((reqs, width), jnp.bfloat16),
             pltpu.VMEM((n, hl + 2, SLOTS, LANES), f32),
@@ -393,7 +433,7 @@
             pltpu.VMEM((n, 2 * chunk_rows, LANES), f32),
             pltpu.VMEM((n, 2 * chunk_rows, LANES), f32),
             pltpu.VMEM((n, 2 * chunk_rows, LANES), f32),
-            pltpu.VMEM((hl, 1, q_rows), f32),
+            pltpu.VMEM((q_rows // LANES, hl, 1, LANES), f32),
             pltpu.VMEM((heads, 8, span), f32),
             pltpu.VMEM((heads, 8, span), f32),
             pltpu.VMEM((2, 8, LANES), f32),
@@ -404,15 +444,16 @@
             dma((n,)), dma((n,)),
             dma((heads,)), dma((heads,)),
             dma((2,)), dma((heads,)),
+            dma((3,)),
         ],
         compiler_params=pltpu.CompilerParams(
-            collective_id=0, has_side_effects=True, vmem_limit_bytes=50 * 1024 * 1024
+            collective_id=0, has_side_effects=True, vmem_limit_bytes=62 * 1024 * 1024
         ),
         cost_estimate=pl.CostEstimate(
             flops=4 * hl * q_rows * ctx_len * HD, bytes_accessed=4 * ctx_len * width,
             transcendentals=hl * q_rows * ctx_len,
         ),
-    )(obs, prefix_keys, prefix_values, dec_query, aux)
+    )(obs, prefix_keys, prefix_values, dec_query, assign, kept, page_counts)
 
 
 def solution(mesh):

time: 67.4 us -> 58.8 us (0.87)
  Pallas kernels: 59.4 us -> 55.2 us
  local copies, waits for them, and re-layouts: 5.75 us -> 2.64 us
  other arithmetic: 1.35 us -> 0 us
    pallas_call x1, Pallas kernels: 59.4 us -> 55.2 us  [local(): pl.pallas_call(functools.partial(kernel, n, heads, side, rows), out_shape...]
    unnamed x12 -> x2, local copies, waits for them, and re-layouts: 5.31 us -> 2.64 us
    select_n x1 -> x0, other arithmetic: 0.69 us -> none  [local(): kept = jnp.where(live, kept_pages[:, 0, :], -1)]
where the time goes in v2:
time: 58.8 us; the launch traced here: 58.5 us
  Pallas kernels  55.2 us (94%)
  local copies, waits for them, and re-layouts  2.64 us (4%)
  between operations  0.64 us (1%)
    pallas_call x1, Pallas kernels, local(): pl.pallas_call(functools.partial(kernel, n, heads, side, rows), out_shape...  55.2 us
    unnamed x2, local copies, waits for them, and re-layouts  2.64 us

profile of v2, /device:TPU:1, one launch (start us, length us, event | category | flops | bytes accessed | tf_op | source)
XLA Modules:
  0.0 58.5 jit_solution(11469604665044623738)
XLA Ops:
  0.6 55.2 %shard_map.86 = (f32[4,512]{1,0:T(4,128)}, bf16[4,2560]{1,0:T(4,128)(2,1)}) custom-call(bf16[16,2560]{1,0:T(8,128)(2,1)} %obs.1, bf16[1024,512]{1,0:T(8,128)(2,1)} %keys_in.1, bf16[1024,512]{1,0:T(8,128)(2,1)} %values_in.1, bf16[64,2560]{1,0:T(8,128)(2,1)} %dec_query_in.1, s32[1,64]{1,0:T(1,128)} %bitcast.5, s32[2,16]{1,0:T(2,128)} %bitcast.4, s32[16,16]{1,0:T(8,128)} %counts.1), custom_call_target="tpu_custom_call" | custom-call | flops 2684354560 | bytes 10485760 | tf_op jit(solution)/shard_map/pallas_call | solution.py:415
  55.9 1.3 %copy.11 = f32[4,512]{1,0:T(4,128)} copy(f32[4,512]{1,0:T(4,128)} %get-tuple-element.4) | data formatting | bytes 16384
  57.2 1.3 %copy.12 = bf16[4,2560]{1,0:T(4,128)(2,1)} copy(bf16[4,2560]{1,0:T(4,128)(2,1)} %get-tuple-element.5) | data formatting | bytes 40960
